TPU v7x, 256 devices: a whole 4x4x8 slice. The times are simulated.
256 devices in a mesh: dp: 4 (over x), seq: 64 (over y, z, core).
Axes of the slice: x: 4, y: 4, z: 8, core: 2. Of those that a mesh axis runs over, the one named last changes fastest.
Arguments:
- bases: int32 [4, 24576], P('dp', 'seq'), may hold values from 0 to 3
- gene_of_stretch: int32 [4, 64], P('dp', 'seq'), may hold values from 0 to 7, never falling along the last dimension, each value on 1 to 32 neighbouring positions
- embed_table: float32 [4, 512], replicated, may hold values from -6 to 6
- kernel_first_block: bfloat16 [11, 512, 512], replicated, may hold values from -0.078125 to 0.078125
- kernel_second_block: bfloat16 [11, 512, 512], replicated, may hold values from -0.078125 to 0.078125
- cotangent: bfloat16 [4, 24576, 512], P('dp', 'seq'), may hold values from -6 to 6
Outputs:
- features: bfloat16 [4, 24576, 512], P('dp', 'seq')
- first_kernel_gradient: float32 [11, 512, 512], P(None, 'seq', 'dp')
- second_kernel_gradient: float32 [11, 512, 512], P(None, 'seq', 'dp')
Inputs may be any that keep to these rules, and one draw needn't show every extreme that they name: `gene_of_stretch`: along each group the gene numbers never fall; each gene covers consecutive stretches, and one gene covers 64 // 2 stretches.
All inputs are finite; a program needn't handle non-finite values.
Results may differ from a plain program's by a relative error of at most 0.0023.
The roundings to bfloat16 on the way count: a program that leaves them out, or rounds other values in their place, can miss the bound.
Values may be sent and summed in bfloat16 or wider, within the bound.
A program may use at most 128 MiB of HBM per device.

v0:
```python
import jax
import jax.numpy as jnp
from jax import lax
from jax.sharding import PartitionSpec as P

KTAP = 11
DILATION_FIRST = 4
DILATION_SECOND = 25


def padded(cells, sides, width):
    for axis, dim in sides:
        count = lax.axis_size(axis)
        ends = count - 1
        head = lax.slice_in_dim(cells, 0, width, axis=dim)
        tail = lax.slice_in_dim(cells, cells.shape[dim] - width, cells.shape[dim], axis=dim)
        cells = jnp.concatenate(
            [
                lax.ppermute(tail, axis, [(i, (i + 1) % count) for i in range(ends)]),
                cells,
                lax.ppermute(head, axis, [((i + 1) % count, i) for i in range(ends)]),
            ],
            axis=dim,
        )
    return cells


def edge_labels(edges, width, row_values):
    return jnp.concatenate(
        [
            jnp.full((width,), edges[0, 0], jnp.int32),
            jnp.full((row_values,), edges[0, 1], jnp.int32),
            jnp.full((width,), edges[0, 2], jnp.int32),
        ]
    )


def taps_stacked_matrix(extended, label_rows, dilation, start, count):
    pieces = []
    own = lax.slice_in_dim(label_rows, start, start + count, axis=0)
    for k in range(KTAP):
        offset = (k - KTAP // 2) * dilation
        source = lax.slice_in_dim(extended, start + offset, start + offset + count, axis=0)
        keep = lax.slice_in_dim(label_rows, start + offset, start + offset + count, axis=0) == own
        pieces.append(jnp.where(keep[:, None], source, jnp.zeros_like(source)))
    return jnp.concatenate(pieces, axis=1)


def embed_rows(base_row, embed_table):
    onehot = (base_row[:, None] == jnp.arange(4, dtype=jnp.int32)[None, :]).astype(jnp.float32)
    return jnp.dot(onehot, embed_table, precision=lax.Precision.HIGHEST).astype(jnp.bfloat16)


def tap_grad(stacked, gradient_list, channels):
    flat = lax.dot_general(
        stacked, gradient_list, (((0,), (0,)), ((), ())), preferred_element_type=jnp.float32
    )
    return flat.reshape(KTAP, channels, channels)


def body(bases, gene_of_stretch, embed_table, kernel_first_block, kernel_second_block, cotangent):
    row_values = bases.shape[1]
    channels = embed_table.shape[1]
    context_first = 5 * DILATION_FIRST
    context_second = 5 * DILATION_SECOND
    edges = padded(gene_of_stretch + 1, (("seq", 1),), 1)
    label_second = edge_labels(edges, context_second, row_values)
    flat_first = kernel_first_block.reshape(KTAP * channels, channels)
    flat_second = kernel_second_block.reshape(KTAP * channels, channels)
    hidden_input = embed_rows(bases[0], embed_table)
    activation_first = jnp.maximum(hidden_input, 0)
    activation_extended = padded(activation_first[None], (("seq", 1),), context_first)[0]
    label_first = edge_labels(edges, context_first, row_values)
    stacked_first = taps_stacked_matrix(
        activation_extended, label_first, DILATION_FIRST, context_first, row_values
    )
    hidden_first = (
        hidden_input.astype(jnp.float32)
        + jnp.dot(stacked_first, flat_first, preferred_element_type=jnp.float32)
    ).astype(jnp.bfloat16)
    activation_second = jnp.maximum(hidden_first, 0)
    activation_broad = padded(activation_second[None], (("seq", 1),), context_second)[0]
    stacked_second = taps_stacked_matrix(
        activation_broad, label_second, DILATION_SECOND, context_second, row_values
    )
    features = (
        hidden_first.astype(jnp.float32)
        + jnp.dot(stacked_second, flat_second, preferred_element_type=jnp.float32)
    ).astype(jnp.bfloat16)
    grads_out = cotangent[0]
    second_term = tap_grad(stacked_second, grads_out, channels)
    gradient_extended = padded(cotangent, (("seq", 1),), context_second)[0]
    stacked_backward = taps_stacked_matrix(
        gradient_extended, label_second, -DILATION_SECOND, context_second, row_values
    )
    backward_second = jnp.einsum(
        "nkc,kic->ni",
        stacked_backward.reshape(row_values, KTAP, channels),
        kernel_second_block,
        preferred_element_type=jnp.float32,
    )
    delta_first = (
        grads_out.astype(jnp.float32) + jnp.where(hidden_first > 0, backward_second, 0.0)
    ).astype(jnp.bfloat16)
    first_term = tap_grad(stacked_first, delta_first, channels)
    first_part, second_part = (
        lax.psum_scatter(first_term, "seq", scatter_dimension=1, tiled=True),
        lax.psum_scatter(second_term, "seq", scatter_dimension=1, tiled=True),
    )
    first_kernel_gradient, second_kernel_gradient = (
        lax.psum_scatter(first_part, "dp", scatter_dimension=2, tiled=True),
        lax.psum_scatter(second_part, "dp", scatter_dimension=2, tiled=True),
    )
    return (features[None], first_kernel_gradient, second_kernel_gradient)


def solution(mesh):
    return jax.shard_map(
        body,
        mesh=mesh,
        in_specs=(P("dp", "seq"), P("dp", "seq"), P(), P(), P(), P("dp", "seq", None)),
        out_specs=(P("dp", "seq", None), P(None, "seq", "dp"), P(None, "seq", "dp")),
        check_vma=False,
    )
```

profile of v0, /device:TPU:1, one launch (start us, length us, event | category | flops | bytes accessed | tf_op | source)
XLA Modules:
  0.0 427.3 jit_solution(14965322157692635805)
XLA Ops:
  7.9 6.1 %collective-permute-start.2 = (s32[1,1]{1,0:T(1,128)}, s32[1,1]{1,0:T(1,128)}, u32[]{:S(2)}, u32[]{:S(2)}) collective-permute-start(s32[1,1]{1,0:T(1,128)} %add.28), channel_id=1, source_target_pairs={{1,0},{2,1},{3,2},{4,3},{5,4},{6,5},{7,6},{8,7},{9,8},{10,9},{11,1... | collective-permute-start | bytes 20 | tf_op jit(solution)/shard_map/ppermute | solution.py:21
  14.0 2.7 collective-permute-start
  16.7 1.0 fusion.134
  17.7 2.4 collective-permute-start.6
  20.1 3.2 collective-permute-start.7
  23.3 0.7 reduce
  24.0 0.5 convolution_convert_fusion
  24.6 2.2 collective-permute-start.1
  26.8 1.0 constant_dynamic-update-slice_fusion.1
  27.8 2.1 collective-permute-start.3
  30.0 0.6 fusion.133
  30.6 0.6 fusion.123
  31.2 0.7 broadcast_in_dim.231
  32.0 0.7 broadcast_in_dim.218
  34.4 1.0 copy-done.3
  35.4 2.4 fusion.2
  38.6 0.2 copy-done.1
  39.7 2.5 fusion.4
  42.1 6.0 %fusion.137 = f32[5632,512]{1,0:T(8,128)} fusion(bf16[384,5632]{1,0:T(8,128)(2,1)S(1)} %fusion.107, bf16[384,512]{1,0:T(8,128)(2,1)S(1)} %fusion.4), kind=kOutput, calls=%fused_computation.211 | convolution fusion | flops 2214592512 | bytes 16252928 | tf_op jit(solution)/shard_map/dot_general | solution.py:55
  48.3 3.4 collective-permute-start.4
  51.8 2.1 collective-permute-start.5
  54.1 0.1 fusion.49
  54.2 0.1 fusion.53
  54.7 3.3 collective-permute-done.5
  58.8 2.1 copy-done.2
  60.9 6.6 %copy.10 = bf16[5632,384]{1,0:T(8,128)(2,1)} copy(bf16[5632,384]{0,1:T(8,128)(2,1)} %bitcast.221) | data formatting | bytes 8650752 | tf_op jit(solution)/shard_map/dot_general | solution.py:55
  67.5 8.5 %fusion.111 = f32[11,512,512]{2,1,0:T(8,128)} fusion(bf16[11,512,384]{2,1,0:T(8,128)(2,1)} %bitcast.220, bf16[1,384,512]{2,1,0:T(8,128)(2,1)S(1)} %copy-done.1), kind=kOutput, calls=%fused_computation.157 | convolution fusion | flops 2214592512 | bytes 16252928 | tf_op jit(solution)/shard_map/dot_general | solution.py:55
  76.1 131.8 %reduce-scatter.5.cloned.1.call-done = f32[11,8,512]{2,1,0:T(8,128)} async-done(((f32[11,512,512]{2,1,0:T(8,128)}), f32[11,8,512]{2,1,0:T(8,128)}) %reduce-scatter.5.cloned.1.call-update) | async-done | bytes 180240 | tf_op jit(solution)/shard_map/reduce_scatter | solution.py:107
  208.0 160.9 %reduce-scatter.9.cloned.1.call-done = f32[11,8,512]{2,1,0:T(8,128)} async-done(((f32[11,512,512]{2,1,0:T(8,128)}), f32[11,8,512]{2,1,0:T(8,128)}) %reduce-scatter.9.cloned.1.call-update) | async-done | bytes 180240 | tf_op jit(solution)/shard_map/reduce_scatter | solution.py:108
  368.9 7.1 %fusion.5 = bf16[1,384,512]{2,1,0:T(8,128)(2,1)} fusion(bf16[384,5632]{1,0:T(8,128)(2,1)} %copy-done.2, bf16[5632,512]{1,0:T(8,128)(2,1)} %bitcast.223, bf16[384,512]{1,0:T(8,128)(2,1)S(1)} %fusion.2), kind=kOutput, calls=%fused_computation.9 | convolution fusion | flops 2215182336 | bytes 10878976 | tf_op jit(solution)/shard_map/dot_general | solution.py:88
  376.0 18.9 %reduce-scatter.7.cloned.1.call-done = f32[11,8,128]{2,1,0:T(8,128)} async-done(((f32[11,8,512]{2,1,0:T(8,128)}), f32[11,8,128]{2,1,0:T(8,128)}) %reduce-scatter.7.cloned.1.call-update) | async-done | bytes 45072 | tf_op jit(solution)/shard_map/reduce_scatter | solution.py:111
  394.8 25.9 %reduce-scatter.11.cloned.1.call-done = f32[11,8,128]{2,1,0:T(8,128)} async-done(((f32[11,8,512]{2,1,0:T(8,128)}), f32[11,8,128]{2,1,0:T(8,128)}) %reduce-scatter.11.cloned.1.call-update) | async-done | bytes 45072 | tf_op jit(solution)/shard_map/reduce_scatter | solution.py:112
  (64 shorter events, 4.7 us)
Async XLA Ops:
  7.2 16.8 %copy-start = (f32[4,512]{1,0:T(4,128)S(1)}, f32[4,512]{1,0:T(4,128)}, u32[]{:S(2)}) copy-start(f32[4,512]{1,0:T(4,128)} %param.8) | copy-start | bytes 24580
  7.2 200.7 %reduce-scatter.5.cloned.1.call-start = ((), (), s32[]{:S(2)}) async-start(), calls=%async_computation.4 | async-start | bytes 11714560 | tf_op jit(solution)/shard_map/reduce_scatter | solution.py:107
  7.9 19.9 %collective-permute-start.2 = (s32[1,1]{1,0:T(1,128)}, s32[1,1]{1,0:T(1,128)}, u32[]{:S(2)}, u32[]{:S(2)}) collective-permute-start(s32[1,1]{1,0:T(1,128)} %add.28), channel_id=1, source_target_pairs={{1,0},{2,1},{3,2},{4,3},{5,4},{6,5},{7,6},{8,7},{9,8},{10,9},{11,1... | collective-permute-start | bytes 20 | tf_op jit(solution)/shard_map/ppermute | solution.py:21
  14.0 17.3 %collective-permute-start = (s32[1,1]{1,0:T(1,128)}, s32[1,1]{1,0:T(1,128)}, u32[]{:S(2)}, u32[]{:S(2)}) collective-permute-start(s32[1,1]{1,0:T(1,128)} %add.28), channel_id=1, source_target_pairs={{0,1},{1,2},{2,3},{3,4},{4,5},{5,6},{6,7},{7,8},{8,9},{9,10},{10,1... | collective-permute-start | bytes 20 | tf_op jit(solution)/shard_map/ppermute | solution.py:19
  17.7 20.2 %collective-permute-start.6 = (bf16[1,125,512]{2,1,0:T(8,128)(2,1)S(1)}, bf16[1,125,512]{2,1,0:T(8,128)(2,1)S(1)}, u32[]{:S(2)}, u32[]{:S(2)}) collective-permute-start(bf16[1,125,512]{2,1,0:T(8,128)(2,1)S(1)} %get-tuple-element.4), channel_id=1, source_target_pairs={{1,0},{2,1},{3,2},{4,3},{5,4},{6,5},{7,6},{8,7},{9,8},{10,9},{11,1... | collective-permute-start | bytes 384008 | tf_op jit(solution)/shard_map/ppermute | solution.py:21
  20.1 18.8 %collective-permute-start.7 = (bf16[1,125,512]{2,1,0:T(8,128)(2,1)S(1)}, bf16[1,125,512]{2,1,0:T(8,128)(2,1)S(1)}, u32[]{:S(2)}, u32[]{:S(2)}) collective-permute-start(bf16[1,125,512]{2,1,0:T(8,128)(2,1)S(1)} %get-tuple-element.3), channel_id=1, source_target_pairs={{0,1},{1,2},{2,3},{3,4},{4,5},{5,6},{6,7},{7,8},{8,9},{9,10},{10,1... | collective-permute-start | bytes 384008 | tf_op jit(solution)/shard_map/ppermute | solution.py:19
  24.6 8.2 %collective-permute-start.1 = (bf16[1,20,512]{2,1,0:T(8,128)(2,1)S(1)}, bf16[1,20,512]{2,1,0:T(8,128)(2,1)S(1)}, u32[]{:S(2)}, u32[]{:S(2)}) collective-permute-start(bf16[1,20,512]{2,1,0:T(8,128)(2,1)S(1)} %get-tuple-element.8), channel_id=1, source_target_pairs={{0,1},{1,2},{2,3},{3,4},{4,5},{5,6},{6,7},{7,8},{8,9},{9,10},{10,1... | collective-permute-start | bytes 61448 | tf_op jit(solution)/shard_map/ppermute | solution.py:19
  27.8 5.8 %collective-permute-start.3 = (bf16[1,20,512]{2,1,0:T(8,128)(2,1)S(1)}, bf16[1,20,512]{2,1,0:T(8,128)(2,1)S(1)}, u32[]{:S(2)}, u32[]{:S(2)}) collective-permute-start(bf16[1,20,512]{2,1,0:T(8,128)(2,1)S(1)} %get-tuple-element.7), channel_id=1, source_target_pairs={{1,0},{2,1},{3,2},{4,3},{5,4},{6,5},{7,6},{8,7},{9,8},{10,9},{11,1... | collective-permute-start | bytes 61448 | tf_op jit(solution)/shard_map/ppermute | solution.py:21
  32.8 2.6 copy-start.3
  34.4 5.2 %slice-start = ((s8[5767168]{0:T(1024)(128)(4,1)}), s8[4194304]{0:T(1024)(128)(4,1)S(1)}, s32[]{:S(2)}) async-start(s8[5767168]{0:T(1024)(128)(4,1)} %bitcast.224), calls=%async_computation.8 | async-start | bytes 8388608
  35.4 4.2 slice-start.1
  37.8 1.0 copy-start.1
  48.2 320.6 %reduce-scatter.9.cloned.1.call-start = ((), (), s32[]{:S(2)}) async-start(), calls=%async_computation.6 | async-start | bytes 11714560 | tf_op jit(solution)/shard_map/reduce_scatter | solution.py:108
  48.3 5.6 %collective-permute-start.4 = (bf16[1,125,512]{2,1,0:T(8,128)(2,1)S(1)}, bf16[1,125,512]{2,1,0:T(8,128)(2,1)S(1)}, u32[]{:S(2)}, u32[]{:S(2)}) collective-permute-start(bf16[1,125,512]{2,1,0:T(8,128)(2,1)S(1)} %get-tuple-element.6), channel_id=1, source_target_pairs={{0,1},{1,2},{2,3},{3,4},{4,5},{5,6},{6,7},{7,8},{8,9},{9,10},{10,1... | collective-permute-start | bytes 384008 | tf_op jit(solution)/shard_map/ppermute | solution.py:19
  51.8 6.3 %collective-permute-start.5 = (bf16[1,125,512]{2,1,0:T(8,128)(2,1)S(1)}, bf16[1,125,512]{2,1,0:T(8,128)(2,1)S(1)}, u32[]{:S(2)}, u32[]{:S(2)}) collective-permute-start(bf16[1,125,512]{2,1,0:T(8,128)(2,1)S(1)} %get-tuple-element.5), channel_id=1, source_target_pairs={{1,0},{2,1},{3,2},{4,3},{5,4},{6,5},{7,6},{8,7},{9,8},{10,9},{11,1... | collective-permute-start | bytes 384008 | tf_op jit(solution)/shard_map/ppermute | solution.py:21
  58.8 2.1 copy-start.2
  76.1 318.8 %reduce-scatter.7.cloned.1.call-start = ((), (), s32[]{:S(2)}) async-start(), calls=%async_computation.5 | async-start | bytes 225280 | tf_op jit(solution)/shard_map/reduce_scatter | solution.py:111
  207.9 212.8 %reduce-scatter.11.cloned.1.call-start = ((), (), s32[]{:S(2)}) async-start(), calls=%async_computation.7 | async-start | bytes 225280 | tf_op jit(solution)/shard_map/reduce_scatter | solution.py:112
Sparse Core Ops, SparseCore 0:
  48.3 159.5 reduce-scatter.4
  212.2 156.6 reduce-scatter.8
  371.9 22.8 reduce-scatter.6
  397.9 22.7 reduce-scatter.10
where the time goes:
time: 429 us; the launch traced here: 427 us
  waiting for transfers between devices  341 us (79%)
  matrix products  27 us (6%)
  starting transfers between devices  24.4 us (6%)
  between operations  14.9 us (3%)
  local copies, waits for them, and re-layouts  13.5 us (3%)
  other arithmetic  6.62 us (2%)
    reduce_scatter x1, waiting for transfers between devices, body(): lax.psum_scatter(second_term, 'seq', scatter_dimension=1, tiled=True)  161 us
    reduce_scatter x1, waiting for transfers between devices, body(): lax.psum_scatter(first_term, 'seq', scatter_dimension=1, tiled=True)  132 us
    reduce_scatter x1, waiting for transfers between devices, body(): lax.psum_scatter(second_part, 'dp', scatter_dimension=2, tiled=True)  25.9 us
    reduce_scatter x1, waiting for transfers between devices, body(): lax.psum_scatter(first_part, 'dp', scatter_dimension=2, tiled=True)  18.9 us
    dot_general x2, matrix products, tap_grad(): lax.dot_general(stacked, gradient_list, (((0,), (0,)), ((), ())), preferr...  14.6 us
    ppermute x4, starting transfers between devices, padded(): lax.ppermute(head, axis, [((i + 1) % count, i) for i in range(ends)])  12.7 us
    ppermute x4, starting transfers between devices, padded(): lax.ppermute(tail, axis, [(i, (i + 1) % count) for i in range(ends)])  11.6 us
  transfers between devices with their start and end apart: 12, of which 5 were waited for; matrix products, arithmetic and copies ran while one was open for 8% of the time, Pallas kernels for 0%

commit v1 on v0

v1 whole, which is shorter than its diff:
```python
import jax
import jax.numpy as jnp
from jax import lax
from jax.experimental import pallas as pl
from jax.experimental.pallas import tpu as pltpu
from jax.sharding import PartitionSpec as P

MESH = pl.DeviceIdType.MESH
KTAP = 11
DILATION_FIRST = 4
DILATION_SECOND = 25
NX, NY, NZ, NC = 4, 4, 8, 2
SEQ = NY * NZ * NC
CH = 512
ROWS = 384
PAD = 128
EXT = ROWS + 2 * PAD
SLICE = CH // (NX * NY)
WIDE = 384
GROUP = NX * NY
HALF = CH // NC
ZROWS = HALF // NZ
F32, BF16 = jnp.float32, jnp.bfloat16


def kernel(
    bases, gene, table, cot, w1_hbm, w2_hbm,
    feat, out1, out2,
    w1, w2, gvm, gf, gt, gbuf, vown, vbuf, tsc, t3, t3t, a1t, ohs, x1b, a2f, acc, fvm,
    st, sbuf, a2s, gs, part, crecv, screcv, zrecv, szrecv, zs, ssum, yrecv, syrecv,
    wsem, w2sem, lsem, hs, hr, vs, vr, gss, gsr, bs, br, ssend, srecv, cs, cr, zsend, zrsem, ys, yr,
):
    x = lax.axis_index("dp")
    seq = lax.axis_index("seq")
    core = seq % NC
    z = (seq // NC) % NZ
    y = seq // (NC * NZ)
    left, right = (seq + SEQ - 1) % SEQ, (seq + 1) % SEQ

    def at(px, py, pz, pc):
        return {"dp": px, "seq": (py * NZ + pz) * NC + pc}

    def remote(src, dst, ssem, rsem, device):
        return pltpu.make_async_remote_copy(
            src_ref=src, dst_ref=dst, send_sem=ssem, recv_sem=rsem, device_id=device, device_id_type=MESH
        )

    load_g = pltpu.make_async_copy(cot.at[0], gvm.at[pl.ds(PAD, ROWS)], lsem.at[0])
    load_g.start()
    load_w1 = [pltpu.make_async_copy(w1_hbm.at[k], w1.at[k], wsem.at[k]) for k in range(KTAP)]
    load_w2 = [pltpu.make_async_copy(w2_hbm.at[k], w2.at[k], w2sem.at[k]) for k in range(KTAP)]
    for copy in load_w1 + load_w2:
        copy.start()

    group = [((x + d // NY) % NX, (y + d % NY) % NY) for d in range(GROUP)]
    partners = [{"dp": x, "seq": left}, {"dp": x, "seq": right}, at(x, y, z, 1 - core)]
    partners += [at(px, py, z, core) for px, py in group[1:]]
    partners += [at(x, y, (z + d) % NZ, core) for d in range(1, NZ)]
    barrier = pltpu.get_barrier_semaphore()
    for device in partners:
        pl.semaphore_signal(barrier, inc=1, device_id=device, device_id_type=MESH)

    label4 = 4.0 * gene[...].astype(F32)
    vown[1] = jnp.broadcast_to(bases[...].astype(F32) + label4, (8, ROWS))
    load_g.wait()
    own_g = gvm[PAD:PAD + ROWS, :]
    gt[...] = own_g.astype(F32).T.astype(BF16)
    pl.semaphore_wait(barrier, len(partners))

    v_copies = [
        remote(vown.at[1], vown.at[0], vs.at[0], vr.at[0], {"dp": x, "seq": right}),
        remote(vown.at[1], vown.at[2], vs.at[1], vr.at[1], {"dp": x, "seq": left}),
    ]
    h_copies = [
        remote(gvm.at[pl.ds(ROWS, PAD)], gvm.at[pl.ds(0, PAD)], hs.at[0], hr.at[0], {"dp": x, "seq": right}),
        remote(gvm.at[pl.ds(PAD, PAD)], gvm.at[pl.ds(PAD + ROWS, PAD)], hs.at[1], hr.at[1], {"dp": x, "seq": left}),
    ]

    def channels_of(px, py):
        return pl.ds(pl.multiple_of(px * (NY * SLICE) + py * SLICE, SLICE), SLICE)

    g_copies = [
        remote(gt.at[channels_of(*group[d])], gbuf.at[d], gss.at[d], gsr.at[d], at(*group[d], z, core))
        for d in range(1, GROUP)
    ]
    for copy in v_copies + h_copies + g_copies:
        copy.start()
    gbuf[0] = gt[channels_of(x, y), :]

    tab = table[...].astype(BF16).astype(F32)
    act = jnp.concatenate([jnp.maximum(tab, 0.0), jnp.zeros((12, CH), F32)], axis=0)
    a1t[...] = act.T
    act = act.astype(BF16)
    tsc[...] = jnp.zeros_like(tsc)
    for k in range(KTAP):
        load_w1[k].wait()
        seen = jnp.dot(act, w1[k], preferred_element_type=F32)
        for b in range(4):
            row = seen[b:b + 1, :]
            if k == KTAP // 2:
                row = row + tab[b:b + 1, :]
            at_row = b * 16 + KTAP - 1 - k
            tsc[at_row:at_row + 1, :] = row
    whole = tsc[...]
    high = whole.astype(BF16).astype(F32)
    middle = (whole - high).astype(BF16).astype(F32)
    low = whole - high - middle
    thirds = jnp.concatenate([high, middle, low], axis=0)
    t3[...] = thirds.astype(BF16)
    turned = thirds.T
    order = [(yy * NZ + zz) * NC + cc for cc in range(NC) for zz in range(NZ) for yy in range(NY)]
    t3t[...] = jnp.concatenate([turned[8 * s:8 * s + 8, :] for s in order], axis=0).astype(BF16)

    for copy in v_copies:
        copy.wait_recv()
    v_left = jnp.where(seq == 0, -64.0, vown[0])
    v_right = jnp.where(seq == SEQ - 1, -64.0, vown[2])
    v_all = jnp.concatenate([v_left, vown[1], v_right], axis=1)
    ahead = PAD + 5 * DILATION_FIRST
    v_all = v_all[0:1, ahead:ahead + 7 * PAD]
    tiles = [v_all[:, PAD * r:PAD * (r + 1)] for r in range(7)]
    vbuf[0] = jnp.concatenate(tiles + [jnp.broadcast_to(label4, (1, PAD))], axis=0)
    b_copies = [
        remote(vbuf.at[0], vbuf.at[d], bs.at[d], br.at[d], at(*group[d], z, core)) for d in range(1, GROUP)
    ]
    for copy in b_copies:
        copy.start()

    def onehot(block):
        lanes = jnp.concatenate([block[r:r + 1, :] for r in range(7)], axis=1)
        own = block[7:8, 0:1]
        shifted = pltpu.roll(jnp.broadcast_to(lanes, (16, 7 * PAD)), 0, 1, stride=DILATION_FIRST, stride_axis=0)
        shifted = shifted[:, PAD:PAD + EXT]
        relative = shifted[5:6, :] - own
        own = jnp.where((relative >= 0.0) & (relative < 4.0), own, 1000.0)
        relative = shifted - own
        return jnp.concatenate([jnp.where(relative == float(b), 1.0, 0.0) for b in range(4)], axis=0)

    own_hot = onehot(vbuf[0])
    hot_rows = own_hot.T
    hot_rows = jnp.concatenate([hot_rows, hot_rows, hot_rows], axis=1).astype(BF16)
    x1 = jnp.dot(hot_rows, t3[...], preferred_element_type=F32).astype(BF16)
    x1b[...] = x1[PAD:PAD + ROWS, :]
    a2f[...] = jnp.maximum(x1.astype(F32), 0.0)

    for copy in h_copies:
        copy.wait_recv()
    keep_left = jnp.where(jnp.floor(v_left[0:1, 0:1] * 0.25) * 4.0 == label4, 1.0, 0.0)
    keep_right = jnp.where(jnp.floor(v_right[0:1, 0:1] * 0.25) * 4.0 == label4, 1.0, 0.0)
    gf[0:PAD, :] = gvm[0:PAD, :].astype(F32) * keep_left
    gf[PAD:PAD + ROWS, :] = own_g.astype(F32)
    gf[PAD + ROWS:, :] = gvm[PAD + ROWS:, :].astype(F32) * keep_right
    for copy in load_w2:
        copy.wait()
    for k in range(KTAP):
        start = PAD - (k - KTAP // 2) * DILATION_SECOND
        term = lax.dot_general(
            gf[start:start + ROWS, :].astype(BF16), w2[k], (((1,), (1,)), ((), ())), preferred_element_type=F32
        )
        acc[...] = term if k == 0 else acc[...] + term
    dx1 = (gf[PAD:PAD + ROWS, :] + jnp.where(x1b[...].astype(F32) > 0.0, acc[...], 0.0)).astype(BF16)
    sums = jnp.dot(own_hot[:, PAD:PAD + ROWS].astype(BF16), dx1, preferred_element_type=F32)
    st[...] = jnp.concatenate([sums, jnp.zeros_like(sums)], axis=0).T
    s_copies = [
        remote(st.at[channels_of(*group[d])], sbuf.at[d], ssend.at[d], srecv.at[d], at(*group[d], z, core))
        for d in range(1, GROUP)
    ]
    for copy in s_copies:
        copy.start()

    for copy in g_copies + b_copies:
        copy.wait_recv()
    gs[...] = jnp.zeros_like(gs)
    part[...] = jnp.zeros_like(part)

    def pair(i, carry):
        for j in range(2):
            slot = 2 * i + j
            hot = onehot(vbuf[slot]).astype(BF16)
            ohs[:, EXT * j:EXT * (j + 1)] = jnp.concatenate([hot, hot, hot], axis=0)
            edge = jnp.zeros((SLICE, PAD), F32)
            wide = jnp.concatenate([edge, gbuf[slot].astype(F32), edge], axis=1)
            for k in range(KTAP):
                shift = (k - KTAP // 2) * DILATION_SECOND
                moved = wide if shift == 0 else pltpu.roll(wide, shift % EXT, 1)
                gs[SLICE * k:SLICE * (k + 1), EXT * j:EXT * (j + 1)] = moved.astype(BF16)
        hidden = jnp.dot(t3t[...], ohs[...], preferred_element_type=F32).astype(BF16)
        a2s[...] = jnp.maximum(hidden, 0)
        part[...] += lax.dot_general(a2s[...], gs[...], (((1,), (1,)), ((), ())), preferred_element_type=F32)
        return carry

    lax.fori_loop(0, GROUP // 2, pair, 0)

    def half_of(c):
        return pl.ds(pl.multiple_of(c * HALF, HALF), HALF)

    c_copy = remote(part.at[half_of(1 - core)], crecv, cs.at[0], cr.at[0], at(x, y, z, 1 - core))
    c_copy.start()
    for copy in s_copies:
        copy.wait_recv()
    group_sum = st[channels_of(x, y), :]
    for d in range(1, GROUP):
        group_sum = group_sum + sbuf[d]
    ssum[0] = group_sum
    sc_copy = remote(ssum.at[0], screcv, cs.at[1], cr.at[1], at(x, y, z, 1 - core))
    sc_copy.start()
    c_copy.wait_recv()
    part[half_of(core), :] += crecv[...]
    sc_copy.wait_recv()
    ssum[1] = ssum[0] + screcv[...]

    def z_rows(pz):
        return pl.ds(pl.multiple_of(core * HALF + pz * ZROWS, ZROWS), ZROWS)

    z_copies, sz_copies = [], []
    for d in range(1, NZ):
        pz = (z + d) % NZ
        z_copies.append(remote(part.at[z_rows(pz)], zrecv.at[d], zsend.at[d], zrsem.at[d], at(x, y, pz, core)))
        sz_copies.append(remote(ssum.at[1], szrecv.at[d], zsend.at[NZ + d], zrsem.at[NZ + d], at(x, y, pz, core)))
    for copy in z_copies + sz_copies:
        copy.start()

    for k in range(KTAP):
        start = PAD + (k - KTAP // 2) * DILATION_SECOND
        term = jnp.dot(a2f[start:start + ROWS, :].astype(BF16), w2[k], preferred_element_type=F32)
        acc[...] = term if k == 0 else acc[...] + term
    fvm[...] = (x1b[...].astype(F32) + acc[...]).astype(BF16)
    store = pltpu.make_async_copy(fvm, feat.at[0], lsem.at[1])
    store.start()

    for copy in z_copies + sz_copies:
        copy.wait_recv()
    total, s_total = part[z_rows(z), :], ssum[1]
    for d in range(1, NZ):
        total, s_total = total + zrecv[d], s_total + szrecv[d]
    zs[...] = total
    ssum[2] = s_total

    y_copies = []
    for d in range(1, NY):
        py = (y + d) % NY
        rows = pl.ds(pl.multiple_of(py * 8, 8), 8)
        y_copies.append(remote(zs.at[rows], yrecv.at[y], ys.at[d], yr.at[d], at(x, py, z, core)))
        y_copies.append(remote(ssum.at[2], syrecv.at[y], ys.at[NY + d], yr.at[NY + d], at(x, py, z, core)))
    for copy in y_copies:
        copy.start()
    yrecv[y] = zs[pl.ds(pl.multiple_of(y * 8, 8), 8), :]
    syrecv[y] = s_total
    for copy in y_copies:
        copy.wait_recv()

    lane = lax.broadcasted_iota(jnp.int32, (8, PAD), 1)
    by_base = jnp.concatenate([syrecv[i] for i in range(NY)], axis=0).T
    rows_act = a1t[pl.ds(pl.multiple_of(seq * 8, 8), 8), :]
    for k in range(KTAP):
        block = jnp.zeros((8, PAD), F32)
        for i in range(NY):
            piece = yrecv[i][:, PAD * (k // NY):PAD * (k // NY) + PAD]
            shift = (SLICE * (i - k % NY)) % PAD
            piece = piece if shift == 0 else pltpu.roll(piece, shift, 1)
            block = jnp.where((lane >= SLICE * i) & (lane < SLICE * (i + 1)), piece, block)
        out2[k] = block
        block = jnp.zeros((8, PAD), F32)
        for b in range(4):
            row = b * 16 + KTAP - 1 - k
            block = block + rows_act[:, b:b + 1] * by_base[row:row + 1, :]
        out1[k] = block

    store.wait()
    for copy in v_copies + h_copies + g_copies + b_copies + s_copies + [c_copy, sc_copy] + z_copies + sz_copies + y_copies:
        copy.wait_send()


def body(bases, gene, table, w1, w2, cotangent):
    vm = lambda *shape, dtype=F32: pltpu.VMEM(shape, dtype)
    dma = lambda n: pltpu.SemaphoreType.DMA((n,))
    vmem = pl.BlockSpec(memory_space=pltpu.VMEM)
    hbm = pl.BlockSpec(memory_space=pl.ANY)
    return pl.pallas_call(
        kernel,
        out_shape=(
            jax.ShapeDtypeStruct((1, ROWS, CH), BF16),
            jax.ShapeDtypeStruct((KTAP, 8, PAD), F32),
            jax.ShapeDtypeStruct((KTAP, 8, PAD), F32),
        ),
        in_specs=[vmem, vmem, vmem, hbm, hbm, hbm],
        out_specs=(hbm, vmem, vmem),
        scratch_shapes=[
            vm(KTAP, CH, CH, dtype=BF16),
            vm(KTAP, CH, CH, dtype=BF16),
            vm(EXT, CH, dtype=BF16),
            vm(EXT, CH),
            vm(CH, ROWS, dtype=BF16),
            vm(GROUP, SLICE, ROWS, dtype=BF16),
            vm(3, 8, ROWS),
            vm(GROUP, 8, PAD),
            vm(64, CH),
            vm(192, CH, dtype=BF16),
            vm(CH, 192, dtype=BF16),
            vm(CH, 16),
            vm(192, 2 * EXT, dtype=BF16),
            vm(ROWS, CH, dtype=BF16),
            vm(EXT, CH),
            vm(ROWS, CH),
            vm(ROWS, CH, dtype=BF16),
            vm(CH, PAD),
            vm(GROUP, SLICE, PAD),
            vm(CH, 2 * EXT, dtype=BF16),
            vm(WIDE, 2 * EXT, dtype=BF16),
            vm(CH, WIDE),
            vm(HALF, WIDE),
            vm(SLICE, PAD),
            vm(NZ, ZROWS, WIDE),
            vm(NZ, SLICE, PAD),
            vm(ZROWS, WIDE),
            vm(3, SLICE, PAD),
            vm(NY, 8, WIDE),
            vm(NY, SLICE, PAD),
            dma(KTAP), dma(KTAP), dma(2),
            dma(2), dma(2), dma(2), dma(2),
            dma(GROUP), dma(GROUP), dma(GROUP), dma(GROUP), dma(GROUP), dma(GROUP),
            dma(2), dma(2), dma(2 * NZ), dma(2 * NZ), dma(2 * NY), dma(2 * NY),
        ],
        compiler_params=pltpu.CompilerParams(
            collective_id=0, has_side_effects=True, vmem_limit_bytes=60 * 1024 * 1024
        ),
    )(bases, gene, table, cotangent, w1, w2)


def solution(mesh):
    return jax.shard_map(
        body,
        mesh=mesh,
        in_specs=(P("dp", "seq"), P("dp", "seq"), P(), P(), P(), P("dp", "seq", None)),
        out_specs=(P("dp", "seq", None), P(None, "seq", "dp"), P(None, "seq", "dp")),
        check_vma=False,
    )
```

time: 429 us -> 60 us (0.14)
  waiting for transfers between devices: 341 us -> 0 us
  Pallas kernels: 0 us -> 53.8 us
  matrix products: 27 us -> 0 us
  starting transfers between devices: 24.4 us -> 0 us
  between operations: 14.9 us -> 1.29 us
  local copies, waits for them, and re-layouts: 13.5 us -> 4.59 us
  other arithmetic: 6.62 us -> 0 us
    reduce_scatter x4 -> x0, waiting for transfers between devices: 337 us -> none  [the longest x1 161 us: body(): lax.psum_scatter(second_term, 'seq', scatter_dimension=1, tiled=True)]
    pallas_call x0 -> x1, Pallas kernels: none -> 53.8 us  [body(): pl.pallas_call(kernel, out_shape=(jax.ShapeDtypeStruct((1, ROWS, CH), BF1...]
    dot_general x6 -> x0, matrix products: 27 us -> none  [the longest x2 14.6 us: tap_grad(): lax.dot_general(stacked, gradient_list, (((0,), (0,)), ((), ())), preferr...]
    ppermute x8 -> x0, starting transfers between devices: 24.3 us -> none  [the longest x4 12.7 us: padded(): lax.ppermute(head, axis, [((i + 1) % count, i) for i in range(ends)])]
    dot_general x1 -> x0, local copies, waits for them, and re-layouts: 6.61 us -> none  [tap_grad(): lax.dot_general(stacked, gradient_list, (((0,), (0,)), ((), ())), preferr...]
    unnamed x31 -> x0, other arithmetic: 4.71 us -> none
  transfers between devices with their start and end apart: 12 -> 0, of which waited for: 5 -> 0; matrix products, arithmetic and copies ran while one was open for 8% -> 0% of each run, Pallas kernels for 0% -> 0%
where the time goes in v1:
time: 60 us; the launch traced here: 59.7 us
  Pallas kernels  53.8 us (90%)
  local copies, waits for them, and re-layouts  4.59 us (8%)
  between operations  1.29 us (2%)
    pallas_call x1, Pallas kernels, body(): pl.pallas_call(kernel, out_shape=(jax.ShapeDtypeStruct((1, ROWS, CH), BF1...  53.8 us
    unnamed x3, local copies, waits for them, and re-layouts  4.59 us

profile of v1, /device:TPU:1, one launch (start us, length us, event | category | flops | bytes accessed | tf_op | source)
XLA Modules:
  0.0 59.7 jit_solution(11247476523312813995)
XLA Ops:
  1.3 53.8 %shard_map.85 = (bf16[1,384,512]{2,1,0:T(8,128)(2,1)}, f32[11,8,128]{2,1,0:T(8,128)}, f32[11,8,128]{2,1,0:T(8,128)}) custom-call(s32[1,384]{1,0:T(1,128)} %bases.1, s32[1,1]{1,0:T(1,128)S(6)} %copy.12.gene, f32[4,512]{1,0:T(4,128)} %table.1, bf16[1,384,512]{2,1,0:T(8,128)(2,1)} %cot.1, bf16[11,512,512]{2,1,0:T(8,128)(2,1)} %w1_hbm.1, ...), custom_call_target="tpu_custom_call" | custom-call | tf_op jit(solution)/shard_map/pallas_call | solution.py:279
  55.1 1.8 %copy.13 = bf16[1,384,512]{2,1,0:T(8,128)(2,1)} copy(bf16[1,384,512]{2,1,0:T(8,128)(2,1)} %get-tuple-element.6) | data formatting | bytes 786432
  56.9 1.4 %copy.14 = f32[11,8,128]{2,1,0:T(8,128)} copy(f32[11,8,128]{2,1,0:T(8,128)} %get-tuple-element.7) | data formatting | bytes 90112
  58.3 1.4 %copy.15 = f32[11,8,128]{2,1,0:T(8,128)} copy(f32[11,8,128]{2,1,0:T(8,128)} %get-tuple-element.8) | data formatting | bytes 90112

commit v2 on v1

--- a/solution.py
+++ b/solution.py
@@ -16,6 +16,7 @@
 PAD = 128
 EXT = ROWS + 2 * PAD
 SLICE = CH // (NX * NY)
+FOLD = SLICE // 2
 WIDE = 384
 GROUP = NX * NY
 HALF = CH // NC
@@ -27,7 +28,7 @@
     bases, gene, table, cot, w1_hbm, w2_hbm,
     feat, out1, out2,
     w1, w2, gvm, gf, gt, gbuf, vown, vbuf, tsc, t3, t3t, a1t, ohs, x1b, a2f, acc, fvm,
-    st, sbuf, a2s, gs, part, crecv, screcv, zrecv, szrecv, zs, ssum, yrecv, syrecv,
+    st, sbuf, a2s, gs, turned_part, part, crecv, screcv, zout, zrecv, szrecv, zs, ssum, yrecv, syrecv,
     wsem, w2sem, lsem, hs, hr, vs, vr, gss, gsr, bs, br, ssend, srecv, cs, cr, zsend, zrsem, ys, yr,
 ):
     x = lax.axis_index("dp")
@@ -49,10 +50,10 @@
     load_g.start()
     load_w1 = [pltpu.make_async_copy(w1_hbm.at[k], w1.at[k], wsem.at[k]) for k in range(KTAP)]
     load_w2 = [pltpu.make_async_copy(w2_hbm.at[k], w2.at[k], w2sem.at[k]) for k in range(KTAP)]
-    for copy in load_w1 + load_w2:
-        copy.start()
-
-    group = [((x + d // NY) % NX, (y + d % NY) % NY) for d in range(GROUP)]
+    for copy in load_w1:
+        copy.start()
+
+    group = [((x + (0, 1, NX - 1, 2)[d // NY]) % NX, (y + d % NY) % NY) for d in range(GROUP)]
     partners = [{"dp": x, "seq": left}, {"dp": x, "seq": right}, at(x, y, z, 1 - core)]
     partners += [at(px, py, z, core) for px, py in group[1:]]
     partners += [at(x, y, (z + d) % NZ, core) for d in range(1, NZ)]
@@ -94,6 +95,7 @@
     tsc[...] = jnp.zeros_like(tsc)
     for k in range(KTAP):
         load_w1[k].wait()
+        load_w2[k].start()
         seen = jnp.dot(act, w1[k], preferred_element_type=F32)
         for b in range(4):
             row = seen[b:b + 1, :]
@@ -107,9 +109,7 @@
     low = whole - high - middle
     thirds = jnp.concatenate([high, middle, low], axis=0)
     t3[...] = thirds.astype(BF16)
-    turned = thirds.T
-    order = [(yy * NZ + zz) * NC + cc for cc in range(NC) for zz in range(NZ) for yy in range(NY)]
-    t3t[...] = jnp.concatenate([turned[8 * s:8 * s + 8, :] for s in order], axis=0).astype(BF16)
+    t3t[...] = thirds.T.astype(BF16)
 
     for copy in v_copies:
         copy.wait_recv()
@@ -160,64 +160,115 @@
         acc[...] = term if k == 0 else acc[...] + term
     dx1 = (gf[PAD:PAD + ROWS, :] + jnp.where(x1b[...].astype(F32) > 0.0, acc[...], 0.0)).astype(BF16)
     sums = jnp.dot(own_hot[:, PAD:PAD + ROWS].astype(BF16), dx1, preferred_element_type=F32)
-    st[...] = jnp.concatenate([sums, jnp.zeros_like(sums)], axis=0).T
+    first = (lax.broadcasted_iota(jnp.int32, sums.shape, 1) & FOLD) == 0
+    sums = jnp.concatenate([jnp.where(first, sums, 0.0), jnp.where(first, 0.0, sums)], axis=0).T
+    folded = [sums[i:i + FOLD, :] + sums[i + FOLD:i + SLICE, :] for i in range(0, CH, SLICE)]
+    st[...] = jnp.concatenate(folded, axis=0)
+
+    def folds_of(px, py):
+        return pl.ds(pl.multiple_of((px * NY + py) * FOLD, FOLD), FOLD)
+
     s_copies = [
-        remote(st.at[channels_of(*group[d])], sbuf.at[d], ssend.at[d], srecv.at[d], at(*group[d], z, core))
+        remote(st.at[folds_of(*group[d])], sbuf.at[d], ssend.at[d], srecv.at[d], at(*group[d], z, core))
         for d in range(1, GROUP)
     ]
     for copy in s_copies:
         copy.start()
 
-    for copy in g_copies + b_copies:
-        copy.wait_recv()
     gs[...] = jnp.zeros_like(gs)
-    part[...] = jnp.zeros_like(part)
+    turned_part[...] = jnp.zeros_like(turned_part)
+    middle_lanes, left_lanes = 2 * ROWS, 2 * (ROWS + PAD)
+
+    def place(ref, rows, j, block, left_too=True, right_too=True):
+        ref[rows, ROWS * j:ROWS * (j + 1)] = block[:, PAD:PAD + ROWS]
+        if left_too:
+            ref[rows, middle_lanes + PAD * j:middle_lanes + PAD * (j + 1)] = block[:, :PAD]
+        if right_too:
+            ref[rows, left_lanes + PAD * j:left_lanes + PAD * (j + 1)] = block[:, PAD + ROWS:]
 
     def pair(i, carry):
         for j in range(2):
             slot = 2 * i + j
             hot = onehot(vbuf[slot]).astype(BF16)
-            ohs[:, EXT * j:EXT * (j + 1)] = jnp.concatenate([hot, hot, hot], axis=0)
+            place(ohs, slice(None), j, jnp.concatenate([hot, hot, hot], axis=0))
             edge = jnp.zeros((SLICE, PAD), F32)
             wide = jnp.concatenate([edge, gbuf[slot].astype(F32), edge], axis=1)
             for k in range(KTAP):
-                shift = (k - KTAP // 2) * DILATION_SECOND
-                moved = wide if shift == 0 else pltpu.roll(wide, shift % EXT, 1)
-                gs[SLICE * k:SLICE * (k + 1), EXT * j:EXT * (j + 1)] = moved.astype(BF16)
-        hidden = jnp.dot(t3t[...], ohs[...], preferred_element_type=F32).astype(BF16)
-        a2s[...] = jnp.maximum(hidden, 0)
-        part[...] += lax.dot_general(a2s[...], gs[...], (((1,), (1,)), ((), ())), preferred_element_type=F32)
+                offset = k - KTAP // 2
+                moved = wide if offset == 0 else pltpu.roll(wide, (offset * DILATION_SECOND) % EXT, 1)
+                place(gs, slice(SLICE * k, SLICE * (k + 1)), j, moved.astype(BF16), offset < 0, offset > 0)
+        hidden = jnp.dot(t3t[...], ohs[...], preferred_element_type=F32)
+        a2s[...] = jnp.maximum(hidden, 0.0).astype(BF16)
+        before, after = SLICE * (KTAP // 2), SLICE * (KTAP // 2 + 1)
+        for rows, lanes in (
+            (slice(0, KTAP * SLICE), slice(0, middle_lanes)),
+            (slice(0, before), slice(middle_lanes, left_lanes)),
+            (slice(after, KTAP * SLICE), slice(left_lanes, 2 * EXT)),
+        ):
+            turned_part[rows, :] += lax.dot_general(
+                gs[rows, lanes], a2s[:, lanes], (((1,), (1,)), ((), ())), preferred_element_type=F32
+            )
         return carry
 
-    lax.fori_loop(0, GROUP // 2, pair, 0)
-
-    def half_of(c):
-        return pl.ds(pl.multiple_of(c * HALF, HALF), HALF)
-
-    c_copy = remote(part.at[half_of(1 - core)], crecv, cs.at[0], cr.at[0], at(x, y, z, 1 - core))
-    c_copy.start()
+    def pairs(first, last):
+        for d in range(max(1, 2 * first), 2 * last):
+            g_copies[d - 1].wait_recv()
+            b_copies[d - 1].wait_recv()
+        lax.fori_loop(first, last, pair, 0)
+
+    pairs(0, 2)
+    pairs(2, 4)
     for copy in s_copies:
         copy.wait_recv()
-    group_sum = st[channels_of(x, y), :]
+    group_sum = st[folds_of(x, y), :]
     for d in range(1, GROUP):
         group_sum = group_sum + sbuf[d]
     ssum[0] = group_sum
     sc_copy = remote(ssum.at[0], screcv, cs.at[1], cr.at[1], at(x, y, z, 1 - core))
     sc_copy.start()
-    c_copy.wait_recv()
-    part[half_of(core), :] += crecv[...]
+    pairs(4, 6)
     sc_copy.wait_recv()
     ssum[1] = ssum[0] + screcv[...]
-
-    def z_rows(pz):
-        return pl.ds(pl.multiple_of(core * HALF + pz * ZROWS, ZROWS), ZROWS)
-
-    z_copies, sz_copies = [], []
+    sz_copies = []
     for d in range(1, NZ):
         pz = (z + d) % NZ
-        z_copies.append(remote(part.at[z_rows(pz)], zrecv.at[d], zsend.at[d], zrsem.at[d], at(x, y, pz, core)))
         sz_copies.append(remote(ssum.at[1], szrecv.at[d], zsend.at[NZ + d], zrsem.at[NZ + d], at(x, y, pz, core)))
-    for copy in z_copies + sz_copies:
+    for copy in sz_copies:
+        copy.start()
+    pairs(6, 8)
+    turned = turned_part[...].T
+    order = [(yy * NZ + zz) * NC + cc for cc in range(NC) for zz in range(NZ) for yy in range(NY)]
+    part[...] = jnp.concatenate([turned[8 * s:8 * s + 8, :] for s in order], axis=0)
+
+    def half_of(c):
+        return pl.ds(pl.multiple_of(c * HALF, HALF), HALF)
+
+    c_copy = remote(part.at[half_of(1 - core)], crecv, cs.at[0], cr.at[0], at(x, y, z, 1 - core))
+    c_copy.start()
+    for copy in sz_copies:
+        copy.wait_recv()
+    s_total = ssum[1]
+    for d in range(1, NZ):
+        s_total = s_total + szrecv[d]
+    ssum[2] = s_total
+    sy_copies = []
+    for d in range(1, NY):
+        py = (y + d) % NY
+        sy_copies.append(remote(ssum.at[2], syrecv.at[y], ys.at[NY + d], yr.at[NY + d], at(x, py, z, core)))
+    for copy in sy_copies:
+        copy.start()
+    syrecv[y] = s_total
+    c_copy.wait_recv()
+    own_half = part[half_of(core), :] + crecv[...]
+    part[half_of(core), :] = own_half
+    zout[...] = own_half.astype(BF16)
+
+    z_copies = []
+    for d in range(1, NZ):
+        pz = (z + d) % NZ
+        rows = pl.ds(pl.multiple_of(pz * ZROWS, ZROWS), ZROWS)
+        z_copies.append(remote(zout.at[rows], zrecv.at[d], zsend.at[d], zrsem.at[d], at(x, y, pz, core)))
+    for copy in z_copies:
         copy.start()
 
     for k in range(KTAP):
@@ -228,29 +279,27 @@
     store = pltpu.make_async_copy(fvm, feat.at[0], lsem.at[1])
     store.start()
 
-    for copy in z_copies + sz_copies:
-        copy.wait_recv()
-    total, s_total = part[z_rows(z), :], ssum[1]
+    for copy in z_copies:
+        copy.wait_recv()
+    total = part[pl.ds(pl.multiple_of(core * HALF + z * ZROWS, ZROWS), ZROWS), :]
     for d in range(1, NZ):
-        total, s_total = total + zrecv[d], s_total + szrecv[d]
+        total = total + zrecv[d].astype(F32)
     zs[...] = total
-    ssum[2] = s_total
 
     y_copies = []
     for d in range(1, NY):
         py = (y + d) % NY
         rows = pl.ds(pl.multiple_of(py * 8, 8), 8)
         y_copies.append(remote(zs.at[rows], yrecv.at[y], ys.at[d], yr.at[d], at(x, py, z, core)))
-        y_copies.append(remote(ssum.at[2], syrecv.at[y], ys.at[NY + d], yr.at[NY + d], at(x, py, z, core)))
     for copy in y_copies:
         copy.start()
     yrecv[y] = zs[pl.ds(pl.multiple_of(y * 8, 8), 8), :]
-    syrecv[y] = s_total
-    for copy in y_copies:
+    for copy in y_copies + sy_copies:
         copy.wait_recv()
 
     lane = lax.broadcasted_iota(jnp.int32, (8, PAD), 1)
-    by_base = jnp.concatenate([syrecv[i] for i in range(NY)], axis=0).T
+    unfolded = [side for i in range(NY) for side in (syrecv[i], pltpu.roll(syrecv[i], PAD // 2, 1))]
+    by_base = jnp.concatenate(unfolded, axis=0).T
     rows_act = a1t[pl.ds(pl.multiple_of(seq * 8, 8), 8), :]
     for k in range(KTAP):
         block = jnp.zeros((8, PAD), F32)
@@ -267,8 +316,15 @@
         out1[k] = block
 
     store.wait()
-    for copy in v_copies + h_copies + g_copies + b_copies + s_copies + [c_copy, sc_copy] + z_copies + sz_copies + y_copies:
+    sent = v_copies + h_copies + g_copies + b_copies + s_copies + [c_copy, sc_copy]
+    for copy in sent + z_copies + sz_copies + y_copies + sy_copies:
         copy.wait_send()
+
+
+def hand_over(feat, grad1, grad2, feat_out, out1, out2):
+    feat_out[...] = feat[...]
+    out1[...] = grad1[...]
+    out2[...] = grad2[...]
 
 
 def body(bases, gene, table, w1, w2, cotangent):
@@ -276,13 +332,14 @@
     dma = lambda n: pltpu.SemaphoreType.DMA((n,))
     vmem = pl.BlockSpec(memory_space=pltpu.VMEM)
     hbm = pl.BlockSpec(memory_space=pl.ANY)
-    return pl.pallas_call(
+    outs = (
+        jax.ShapeDtypeStruct((1, ROWS, CH), BF16),
+        jax.ShapeDtypeStruct((KTAP, 8, PAD), F32),
+        jax.ShapeDtypeStruct((KTAP, 8, PAD), F32),
+    )
+    results = pl.pallas_call(
         kernel,
-        out_shape=(
-            jax.ShapeDtypeStruct((1, ROWS, CH), BF16),
-            jax.ShapeDtypeStruct((KTAP, 8, PAD), F32),
-            jax.ShapeDtypeStruct((KTAP, 8, PAD), F32),
-        ),
+        out_shape=outs,
         in_specs=[vmem, vmem, vmem, hbm, hbm, hbm],
         out_specs=(hbm, vmem, vmem),
         scratch_shapes=[
@@ -303,19 +360,21 @@
             vm(EXT, CH),
             vm(ROWS, CH),
             vm(ROWS, CH, dtype=BF16),
-            vm(CH, PAD),
-            vm(GROUP, SLICE, PAD),
+            vm(CH // 2, PAD),
+            vm(GROUP, FOLD, PAD),
             vm(CH, 2 * EXT, dtype=BF16),
             vm(WIDE, 2 * EXT, dtype=BF16),
+            vm(WIDE, CH),
             vm(CH, WIDE),
             vm(HALF, WIDE),
-            vm(SLICE, PAD),
-            vm(NZ, ZROWS, WIDE),
-            vm(NZ, SLICE, PAD),
+            vm(FOLD, PAD),
+            vm(HALF, WIDE, dtype=BF16),
+            vm(NZ, ZROWS, WIDE, dtype=BF16),
+            vm(NZ, FOLD, PAD),
             vm(ZROWS, WIDE),
-            vm(3, SLICE, PAD),
+            vm(3, FOLD, PAD),
             vm(NY, 8, WIDE),
-            vm(NY, SLICE, PAD),
+            vm(NY, FOLD, PAD),
             dma(KTAP), dma(KTAP), dma(2),
             dma(2), dma(2), dma(2), dma(2),
             dma(GROUP), dma(GROUP), dma(GROUP), dma(GROUP), dma(GROUP), dma(GROUP),
@@ -325,6 +384,12 @@
             collective_id=0, has_side_effects=True, vmem_limit_bytes=60 * 1024 * 1024
         ),
     )(bases, gene, table, cotangent, w1, w2)
+    return pl.pallas_call(
+        hand_over,
+        out_shape=outs,
+        in_specs=[vmem, vmem, vmem],
+        out_specs=(vmem, vmem, vmem),
+    )(*results)
 
 
 def solution(mesh):

time: 60 us -> 47.1 us (0.79)
  the two profiles are of different devices: /device:TPU:1 before, /device:TPU:2 now
where the time goes in v2:
time: 47.1 us; the launch traced here: 47 us
  Pallas kernels  45.7 us (97%)
  between operations  1.28 us (3%)
    pallas_call x1, Pallas kernels, body(): pl.pallas_call(kernel, out_shape=outs, in_specs=[vmem, vmem, vmem, hbm, h...  43.9 us
    pallas_call x1, Pallas kernels, body(): pl.pallas_call(hand_over, out_shape=outs, in_specs=[vmem, vmem, vmem], ou...  1.8 us

profile of v2, /device:TPU:2, one launch (start us, length us, event | category | flops | bytes accessed | tf_op | source)
XLA Modules:
  0.0 47.0 jit_solution(15250308894415862315)
XLA Ops:
  1.3 43.9 %shard_map.85 = (bf16[1,384,512]{2,1,0:T(8,128)(2,1)}, f32[11,8,128]{2,1,0:T(8,128)}, f32[11,8,128]{2,1,0:T(8,128)}) custom-call(s32[1,384]{1,0:T(1,128)} %bases.1, s32[1,1]{1,0:T(1,128)S(6)} %copy.9.gene, f32[4,512]{1,0:T(4,128)} %table.1, bf16[1,384,512]{2,1,0:T(8,128)(2,1)} %cot.1, bf16[11,512,512]{2,1,0:T(8,128)(2,1)} %w1_hbm.1, bf16[11,512,512]{2,1,0:T(8,128)(2,1)} %w2_hbm.1), custom_call_target="tpu_custom_call" | custom-call | tf_op jit(solution)/shard_map/pallas_call | solution.py:340
  45.2 1.8 %shard_map.86 = (bf16[1,384,512]{2,1,0:T(8,128)(2,1)}, f32[11,8,128]{2,1,0:T(8,128)}, f32[11,8,128]{2,1,0:T(8,128)}) custom-call(bf16[1,384,512]{2,1,0:T(8,128)(2,1)} %get-tuple-element.6.feat, f32[11,8,128]{2,1,0:T(8,128)} %get-tuple-element.7.grad1, f32[11,8,128]{2,1,0:T(8,128)} %get-tuple-element.8.grad2), custom_call_target="tpu_custom_call" | custom-call | tf_op jit(solution)/shard_map/pallas_call | solution.py:387

commit v3 on v2

--- a/solution.py
+++ b/solution.py
@@ -21,15 +21,16 @@
 GROUP = NX * NY
 HALF = CH // NC
 ZROWS = HALF // NZ
+SHARE = (KTAP + 1) // NC
 F32, BF16 = jnp.float32, jnp.bfloat16
 
 
 def kernel(
-    bases, gene, table, cot, w1_hbm, w2_hbm,
+    bases_in, gene_in, table_in, cot, w1_hbm, w2_hbm,
     feat, out1, out2,
-    w1, w2, gvm, gf, gt, gbuf, vown, vbuf, tsc, t3, t3t, a1t, ohs, x1b, a2f, acc, fvm,
+    bases, gene, table, w1, w2, tmine, tother, gvm, gf, gt, gbuf, vown, vbuf, tsc, t3, t3t, a1t, ohs, x1b, a2f, acc, fvm,
     st, sbuf, a2s, gs, turned_part, part, crecv, screcv, zout, zrecv, szrecv, zs, ssum, yrecv, syrecv,
-    wsem, w2sem, lsem, hs, hr, vs, vr, gss, gsr, bs, br, ssend, srecv, cs, cr, zsend, zrsem, ys, yr,
+    wsem, w2sem, lsem, ts, tr, hs, hr, vs, vr, gss, gsr, bs, br, ssend, srecv, cs, cr, zsend, zrsem, ys, yr,
 ):
     x = lax.axis_index("dp")
     seq = lax.axis_index("seq")
@@ -46,13 +47,6 @@
             src_ref=src, dst_ref=dst, send_sem=ssem, recv_sem=rsem, device_id=device, device_id_type=MESH
         )
 
-    load_g = pltpu.make_async_copy(cot.at[0], gvm.at[pl.ds(PAD, ROWS)], lsem.at[0])
-    load_g.start()
-    load_w1 = [pltpu.make_async_copy(w1_hbm.at[k], w1.at[k], wsem.at[k]) for k in range(KTAP)]
-    load_w2 = [pltpu.make_async_copy(w2_hbm.at[k], w2.at[k], w2sem.at[k]) for k in range(KTAP)]
-    for copy in load_w1:
-        copy.start()
-
     group = [((x + (0, 1, NX - 1, 2)[d // NY]) % NX, (y + d % NY) % NY) for d in range(GROUP)]
     partners = [{"dp": x, "seq": left}, {"dp": x, "seq": right}, at(x, y, z, 1 - core)]
     partners += [at(px, py, z, core) for px, py in group[1:]]
@@ -61,6 +55,18 @@
     for device in partners:
         pl.semaphore_signal(barrier, inc=1, device_id=device, device_id_type=MESH)
 
+    small = [
+        pltpu.make_async_copy(src, dst, lsem.at[2 + i])
+        for i, (src, dst) in enumerate(((bases_in, bases), (gene_in, gene), (table_in, table)))
+    ]
+    load_g = pltpu.make_async_copy(cot.at[0], gvm.at[pl.ds(PAD, ROWS)], lsem.at[0])
+    load_w1 = [pltpu.make_async_copy(w1_hbm.at[core * (SHARE - 1) + i], w1.at[i], wsem.at[i]) for i in range(SHARE)]
+    load_w2 = [pltpu.make_async_copy(w2_hbm.at[k], w2.at[k], w2sem.at[k]) for k in range(KTAP)]
+    for copy in small + [load_g] + load_w1:
+        copy.start()
+
+    for copy in small:
+        copy.wait()
     label4 = 4.0 * gene[...].astype(F32)
     vown[1] = jnp.broadcast_to(bases[...].astype(F32) + label4, (8, ROWS))
     load_g.wait()
@@ -92,11 +98,58 @@
     act = jnp.concatenate([jnp.maximum(tab, 0.0), jnp.zeros((12, CH), F32)], axis=0)
     a1t[...] = act.T
     act = act.astype(BF16)
+    for i in range(SHARE):
+        load_w1[i].wait()
+        for copy in load_w2[2 * i:2 * i + 2]:
+            copy.start()
+        tmine[i] = jnp.dot(act, w1[i], preferred_element_type=F32)[0:8, :]
+    t_copy = remote(tmine, tother, ts.at[0], tr.at[0], at(x, y, z, 1 - core))
+    t_copy.start()
+
+    for copy in v_copies:
+        copy.wait_recv()
+    v_left = jnp.where(seq == 0, -64.0, vown[0])
+    v_right = jnp.where(seq == SEQ - 1, -64.0, vown[2])
+    v_all = jnp.concatenate([v_left, vown[1], v_right], axis=1)
+    ahead = PAD + 5 * DILATION_FIRST
+    v_all = v_all[0:1, ahead:ahead + 7 * PAD]
+    tiles = [v_all[:, PAD * r:PAD * (r + 1)] for r in range(7)]
+    vbuf[0] = jnp.concatenate(tiles + [jnp.broadcast_to(label4, (1, PAD))], axis=0)
+    b_copies = [
+        remote(vbuf.at[0], vbuf.at[d], bs.at[d], br.at[d], at(*group[d], z, core)) for d in range(1, GROUP)
+    ]
+    for copy in b_copies:
+        copy.start()
+
+    def onehot(block):
+        lanes = jnp.concatenate([block[r:r + 1, :] for r in range(7)], axis=1)
+        own = block[7:8, 0:1]
+        shifted = pltpu.roll(jnp.broadcast_to(lanes, (16, 7 * PAD)), 0, 1, stride=DILATION_FIRST, stride_axis=0)
+        shifted = shifted[:, PAD:PAD + EXT]
+        relative = shifted[5:6, :] - own
+        own = jnp.where((relative >= 0.0) & (relative < 4.0), own, 1000.0)
+        relative = shifted - own
+        return jnp.concatenate([jnp.where(relative == float(b), 1.0, 0.0) for b in range(4)], axis=0)
+
+    for copy in h_copies:
+        copy.wait_recv()
+    keep_left = jnp.where(jnp.floor(v_left[0:1, 0:1] * 0.25) * 4.0 == label4, 1.0, 0.0)
+    keep_right = jnp.where(jnp.floor(v_right[0:1, 0:1] * 0.25) * 4.0 == label4, 1.0, 0.0)
+    gf[0:PAD, :] = gvm[0:PAD, :].astype(F32) * keep_left
+    gf[PAD:PAD + ROWS, :] = own_g.astype(F32)
+    gf[PAD + ROWS:, :] = gvm[PAD + ROWS:, :].astype(F32) * keep_right
+    for k in range(KTAP):
+        load_w2[k].wait()
+        start = PAD - (k - KTAP // 2) * DILATION_SECOND
+        term = lax.dot_general(
+            gf[start:start + ROWS, :].astype(BF16), w2[k], (((1,), (1,)), ((), ())), preferred_element_type=F32
+        )
+        acc[...] = term if k == 0 else acc[...] + term
+    t_copy.wait_recv()
     tsc[...] = jnp.zeros_like(tsc)
     for k in range(KTAP):
-        load_w1[k].wait()
-        load_w2[k].start()
-        seen = jnp.dot(act, w1[k], preferred_element_type=F32)
+        i = k if k < SHARE else k - SHARE + 1
+        seen = jnp.where(core == (0 if k < SHARE else 1), tmine[i], tother[i])
         for b in range(4):
             row = seen[b:b + 1, :]
             if k == KTAP // 2:
@@ -111,31 +164,6 @@
     t3[...] = thirds.astype(BF16)
     t3t[...] = thirds.T.astype(BF16)
 
-    for copy in v_copies:
-        copy.wait_recv()
-    v_left = jnp.where(seq == 0, -64.0, vown[0])
-    v_right = jnp.where(seq == SEQ - 1, -64.0, vown[2])
-    v_all = jnp.concatenate([v_left, vown[1], v_right], axis=1)
-    ahead = PAD + 5 * DILATION_FIRST
-    v_all = v_all[0:1, ahead:ahead + 7 * PAD]
-    tiles = [v_all[:, PAD * r:PAD * (r + 1)] for r in range(7)]
-    vbuf[0] = jnp.concatenate(tiles + [jnp.broadcast_to(label4, (1, PAD))], axis=0)
-    b_copies = [
-        remote(vbuf.at[0], vbuf.at[d], bs.at[d], br.at[d], at(*group[d], z, core)) for d in range(1, GROUP)
-    ]
-    for copy in b_copies:
-        copy.start()
-
-    def onehot(block):
-        lanes = jnp.concatenate([block[r:r + 1, :] for r in range(7)], axis=1)
-        own = block[7:8, 0:1]
-        shifted = pltpu.roll(jnp.broadcast_to(lanes, (16, 7 * PAD)), 0, 1, stride=DILATION_FIRST, stride_axis=0)
-        shifted = shifted[:, PAD:PAD + EXT]
-        relative = shifted[5:6, :] - own
-        own = jnp.where((relative >= 0.0) & (relative < 4.0), own, 1000.0)
-        relative = shifted - own
-        return jnp.concatenate([jnp.where(relative == float(b), 1.0, 0.0) for b in range(4)], axis=0)
-
     own_hot = onehot(vbuf[0])
     hot_rows = own_hot.T
     hot_rows = jnp.concatenate([hot_rows, hot_rows, hot_rows], axis=1).astype(BF16)
@@ -143,21 +171,6 @@
     x1b[...] = x1[PAD:PAD + ROWS, :]
     a2f[...] = jnp.maximum(x1.astype(F32), 0.0)
 
-    for copy in h_copies:
-        copy.wait_recv()
-    keep_left = jnp.where(jnp.floor(v_left[0:1, 0:1] * 0.25) * 4.0 == label4, 1.0, 0.0)
-    keep_right = jnp.where(jnp.floor(v_right[0:1, 0:1] * 0.25) * 4.0 == label4, 1.0, 0.0)
-    gf[0:PAD, :] = gvm[0:PAD, :].astype(F32) * keep_left
-    gf[PAD:PAD + ROWS, :] = own_g.astype(F32)
-    gf[PAD + ROWS:, :] = gvm[PAD + ROWS:, :].astype(F32) * keep_right
-    for copy in load_w2:
-        copy.wait()
-    for k in range(KTAP):
-        start = PAD - (k - KTAP // 2) * DILATION_SECOND
-        term = lax.dot_general(
-            gf[start:start + ROWS, :].astype(BF16), w2[k], (((1,), (1,)), ((), ())), preferred_element_type=F32
-        )
-        acc[...] = term if k == 0 else acc[...] + term
     dx1 = (gf[PAD:PAD + ROWS, :] + jnp.where(x1b[...].astype(F32) > 0.0, acc[...], 0.0)).astype(BF16)
     sums = jnp.dot(own_hot[:, PAD:PAD + ROWS].astype(BF16), dx1, preferred_element_type=F32)
     first = (lax.broadcasted_iota(jnp.int32, sums.shape, 1) & FOLD) == 0
@@ -218,6 +231,7 @@
 
     pairs(0, 2)
     pairs(2, 4)
+    pairs(4, 6)
     for copy in s_copies:
         copy.wait_recv()
     group_sum = st[folds_of(x, y), :]
@@ -226,7 +240,7 @@
     ssum[0] = group_sum
     sc_copy = remote(ssum.at[0], screcv, cs.at[1], cr.at[1], at(x, y, z, 1 - core))
     sc_copy.start()
-    pairs(4, 6)
+    pairs(6, 7)
     sc_copy.wait_recv()
     ssum[1] = ssum[0] + screcv[...]
     sz_copies = []
@@ -235,7 +249,7 @@
         sz_copies.append(remote(ssum.at[1], szrecv.at[d], zsend.at[NZ + d], zrsem.at[NZ + d], at(x, y, pz, core)))
     for copy in sz_copies:
         copy.start()
-    pairs(6, 8)
+    pairs(7, 8)
     turned = turned_part[...].T
     order = [(yy * NZ + zz) * NC + cc for cc in range(NC) for zz in range(NZ) for yy in range(NY)]
     part[...] = jnp.concatenate([turned[8 * s:8 * s + 8, :] for s in order], axis=0)
@@ -245,6 +259,27 @@
 
     c_copy = remote(part.at[half_of(1 - core)], crecv, cs.at[0], cr.at[0], at(x, y, z, 1 - core))
     c_copy.start()
+    c_copy.wait_recv()
+    own_half = part[half_of(core), :] + crecv[...]
+    part[half_of(core), :] = own_half
+    zout[...] = own_half.astype(BF16)
+
+    z_copies = []
+    for d in range(1, NZ):
+        pz = (z + d) % NZ
+        rows = pl.ds(pl.multiple_of(pz * ZROWS, ZROWS), ZROWS)
+        z_copies.append(remote(zout.at[rows], zrecv.at[d], zsend.at[d], zrsem.at[d], at(x, y, pz, core)))
+    for copy in z_copies:
+        copy.start()
+
+    for k in range(KTAP):
+        start = PAD + (k - KTAP // 2) * DILATION_SECOND
+        term = jnp.dot(a2f[start:start + ROWS, :].astype(BF16), w2[k], preferred_element_type=F32)
+        acc[...] = term if k == 0 else acc[...] + term
+    fvm[...] = (x1b[...].astype(F32) + acc[...]).astype(BF16)
+    store = pltpu.make_async_copy(fvm, feat.at[0], lsem.at[1])
+    store.start()
+
     for copy in sz_copies:
         copy.wait_recv()
     s_total = ssum[1]
@@ -258,33 +293,13 @@
     for copy in sy_copies:
         copy.start()
     syrecv[y] = s_total
-    c_copy.wait_recv()
-    own_half = part[half_of(core), :] + crecv[...]
-    part[half_of(core), :] = own_half
-    zout[...] = own_half.astype(BF16)
-
-    z_copies = []
-    for d in range(1, NZ):
-        pz = (z + d) % NZ
-        rows = pl.ds(pl.multiple_of(pz * ZROWS, ZROWS), ZROWS)
-        z_copies.append(remote(zout.at[rows], zrecv.at[d], zsend.at[d], zrsem.at[d], at(x, y, pz, core)))
-    for copy in z_copies:
-        copy.start()
-
-    for k in range(KTAP):
-        start = PAD + (k - KTAP // 2) * DILATION_SECOND
-        term = jnp.dot(a2f[start:start + ROWS, :].astype(BF16), w2[k], preferred_element_type=F32)
-        acc[...] = term if k == 0 else acc[...] + term
-    fvm[...] = (x1b[...].astype(F32) + acc[...]).astype(BF16)
-    store = pltpu.make_async_copy(fvm, feat.at[0], lsem.at[1])
-    store.start()
-
     for copy in z_copies:
         copy.wait_recv()
     total = part[pl.ds(pl.multiple_of(core * HALF + z * ZROWS, ZROWS), ZROWS), :]
     for d in range(1, NZ):
         total = total + zrecv[d].astype(F32)
     zs[...] = total
+
 
     y_copies = []
     for d in range(1, NY):
@@ -316,7 +331,7 @@
         out1[k] = block
 
     store.wait()
-    sent = v_copies + h_copies + g_copies + b_copies + s_copies + [c_copy, sc_copy]
+    sent = v_copies + h_copies + g_copies + b_copies + s_copies + [t_copy, c_copy, sc_copy]
     for copy in sent + z_copies + sz_copies + y_copies + sy_copies:
         copy.wait_send()
 
@@ -340,11 +355,16 @@
     results = pl.pallas_call(
         kernel,
         out_shape=outs,
-        in_specs=[vmem, vmem, vmem, hbm, hbm, hbm],
+        in_specs=[hbm] * 6,
         out_specs=(hbm, vmem, vmem),
         scratch_shapes=[
+            vm(1, ROWS, dtype=jnp.int32),
+            vm(1, 1, dtype=jnp.int32),
+            vm(4, CH),
+            vm(SHARE, CH, CH, dtype=BF16),
             vm(KTAP, CH, CH, dtype=BF16),
-            vm(KTAP, CH, CH, dtype=BF16),
+            vm(SHARE, 8, CH),
+            vm(SHARE, 8, CH),
             vm(EXT, CH, dtype=BF16),
             vm(EXT, CH),
             vm(CH, ROWS, dtype=BF16),
@@ -375,7 +395,7 @@
             vm(3, FOLD, PAD),
             vm(NY, 8, WIDE),
             vm(NY, FOLD, PAD),
-            dma(KTAP), dma(KTAP), dma(2),
+            dma(SHARE), dma(KTAP), dma(5), dma(1), dma(1),
             dma(2), dma(2), dma(2), dma(2),
             dma(GROUP), dma(GROUP), dma(GROUP), dma(GROUP), dma(GROUP), dma(GROUP),
             dma(2), dma(2), dma(2 * NZ), dma(2 * NZ), dma(2 * NY), dma(2 * NY),

time: 47.1 us -> 45 us (0.955)
  the two profiles are of different devices: /device:TPU:2 before, /device:TPU:1 now
where the time goes in v3:
time: 45 us; the launch traced here: 44.1 us
  Pallas kernels  42.8 us (95%)
  between operations  1.28 us (3%)
    pallas_call x1, Pallas kernels, body(): pl.pallas_call(kernel, out_shape=outs, in_specs=[hbm] * 6, out_specs=(hbm...  41 us
    pallas_call x1, Pallas kernels, body(): pl.pallas_call(hand_over, out_shape=outs, in_specs=[vmem, vmem, vmem], ou...  1.8 us

profile of v3, /device:TPU:1, one launch (start us, length us, event | category | flops | bytes accessed | tf_op | source)
XLA Modules:
  0.0 44.1 jit_solution(7631792105893515040)
XLA Ops:
  1.3 41.0 %shard_map.85 = (bf16[1,384,512]{2,1,0:T(8,128)(2,1)}, f32[11,8,128]{2,1,0:T(8,128)}, f32[11,8,128]{2,1,0:T(8,128)}) custom-call(s32[1,384]{1,0:T(1,128)} %bases_in.1, s32[1,1]{1,0:T(1,128)S(6)} %copy.9.gene_in, f32[4,512]{1,0:T(4,128)} %table_in.1, bf16[1,384,512]{2,1,0:T(8,128)(2,1)} %cot.1, bf16[11,512,512]{2,1,0:T(8,128)(2,1)} %w1_hbm.1, ...), custom_call_target="tpu_custom_call" | custom-call | tf_op jit(solution)/shard_map/pallas_call | solution.py:355
  42.3 1.8 %shard_map.86 = (bf16[1,384,512]{2,1,0:T(8,128)(2,1)}, f32[11,8,128]{2,1,0:T(8,128)}, f32[11,8,128]{2,1,0:T(8,128)}) custom-call(bf16[1,384,512]{2,1,0:T(8,128)(2,1)} %get-tuple-element.6.feat, f32[11,8,128]{2,1,0:T(8,128)} %get-tuple-element.7.grad1, f32[11,8,128]{2,1,0:T(8,128)} %get-tuple-element.8.grad2), custom_call_target="tpu_custom_call" | custom-call | tf_op jit(solution)/shard_map/pallas_call | solution.py:407

commit v4 on v3

--- a/solution.py
+++ b/solution.py
@@ -90,7 +90,7 @@
         remote(gt.at[channels_of(*group[d])], gbuf.at[d], gss.at[d], gsr.at[d], at(*group[d], z, core))
         for d in range(1, GROUP)
     ]
-    for copy in v_copies + h_copies + g_copies:
+    for copy in v_copies + h_copies:
         copy.start()
     gbuf[0] = gt[channels_of(x, y), :]
 
@@ -98,13 +98,17 @@
     act = jnp.concatenate([jnp.maximum(tab, 0.0), jnp.zeros((12, CH), F32)], axis=0)
     a1t[...] = act.T
     act = act.astype(BF16)
-    for i in range(SHARE):
+    def share(i):
         load_w1[i].wait()
         for copy in load_w2[2 * i:2 * i + 2]:
             copy.start()
         tmine[i] = jnp.dot(act, w1[i], preferred_element_type=F32)[0:8, :]
-    t_copy = remote(tmine, tother, ts.at[0], tr.at[0], at(x, y, z, 1 - core))
-    t_copy.start()
+        if i == 0:
+            for copy in g_copies:
+                copy.start()
+
+    share(0)
+    share(1)
 
     for copy in v_copies:
         copy.wait_recv()
@@ -120,6 +124,11 @@
     ]
     for copy in b_copies:
         copy.start()
+
+    for i in range(2, SHARE):
+        share(i)
+    t_copy = remote(tmine, tother, ts.at[0], tr.at[0], at(x, y, z, 1 - core))
+    t_copy.start()
 
     def onehot(block):
         lanes = jnp.concatenate([block[r:r + 1, :] for r in range(7)], axis=1)

time: 45 us -> 44.8 us (level)
  no operation moved by 1% of the time
where the time goes in v4:
time: 44.8 us; the launch traced here: 44.1 us
  Pallas kernels  42.8 us (96%)
  between operations  1.28 us (3%)
    pallas_call x1, Pallas kernels, body(): pl.pallas_call(kernel, out_shape=outs, in_specs=[hbm] * 6, out_specs=(hbm...  41 us
    pallas_call x1, Pallas kernels, body(): pl.pallas_call(hand_over, out_shape=outs, in_specs=[vmem, vmem, vmem], ou...  1.8 us

profile of v4, /device:TPU:1, one launch (start us, length us, event | category | flops | bytes accessed | tf_op | source)
XLA Modules:
  0.0 44.1 jit_solution(10793749744987434914)
XLA Ops:
  1.3 41.0 %shard_map.85 = (bf16[1,384,512]{2,1,0:T(8,128)(2,1)}, f32[11,8,128]{2,1,0:T(8,128)}, f32[11,8,128]{2,1,0:T(8,128)}) custom-call(s32[1,384]{1,0:T(1,128)} %bases_in.1, s32[1,1]{1,0:T(1,128)S(6)} %copy.9.gene_in, f32[4,512]{1,0:T(4,128)} %table_in.1, bf16[1,384,512]{2,1,0:T(8,128)(2,1)} %cot.1, bf16[11,512,512]{2,1,0:T(8,128)(2,1)} %w1_hbm.1, ...), custom_call_target="tpu_custom_call" | custom-call | tf_op jit(solution)/shard_map/pallas_call | solution.py:364
  42.3 1.8 %shard_map.86 = (bf16[1,384,512]{2,1,0:T(8,128)(2,1)}, f32[11,8,128]{2,1,0:T(8,128)}, f32[11,8,128]{2,1,0:T(8,128)}) custom-call(bf16[1,384,512]{2,1,0:T(8,128)(2,1)} %get-tuple-element.6.feat, f32[11,8,128]{2,1,0:T(8,128)} %get-tuple-element.7.grad1, f32[11,8,128]{2,1,0:T(8,128)} %get-tuple-element.8.grad2), custom_call_target="tpu_custom_call" | custom-call | tf_op jit(solution)/shard_map/pallas_call | solution.py:416
